TPU v7x, 32 devices: a whole 2x2x4 slice. The times are simulated.
32 devices in a mesh: chan: 8 (over z, x), win: 4 (over y, core).
Axes of the slice: x: 2, y: 2, z: 4, core: 2. Of those that a mesh axis runs over, the one named last changes fastest.
Arguments:
- spectra: bfloat16 [2, 8, 512, 1024], P(None, 'win', 'chan'), may hold values from -200 to 200
- pair_blocks: int32 [32, 2], P(('chan', 'win')), may hold values from 0 to 7, as said below
Outputs:
- stacks: float32 [32, 64, 64, 256], P(('chan', 'win'))
Inputs may be any that keep to these rules, and one draw needn't show every extreme that they name: `pair_blocks`: row p belongs to channel block c = p // 4. The 4 rows of c hold, in a drawn order and each in a drawn orientation, the pairs of blocks c - d // 2 and c - d // 2 + d for d = 0 to 3, block numbers taken modulo 8; so every pair of blocks at cyclic distance below 4 appears exactly once in all.
All inputs are finite; a program needn't handle non-finite values.
Results may differ from a plain program's by a relative error of at most 0.0032.
Values may be sent and summed in bfloat16 or wider, within the bound.
A program may use at most 256 MiB of HBM per device.

v0:
```python
import functools
import math

import jax
import jax.numpy as jnp
import ml_dtypes
import numpy as np
from jax import lax
from jax.experimental import pallas as pl
from jax.experimental.pallas import tpu as pltpu
from jax.sharding import PartitionSpec as P

NLAG = 256
HALF_BAND = 64
MESH = pl.DeviceIdType.MESH

eps = 1e-05
first_bin = 60.0
samples = 15000.0

CORES = 2
TILE = 8
QUADS = 4


def smoothing(length_bins, half_width):
    indices = jnp.arange(length_bins, dtype=jnp.int32)
    return (jnp.abs(indices[:, None] - indices[None, :]) <= half_width).astype(jnp.float32)


def whiten(spectra):
    length_bins = spectra.shape[-1]
    real_part = spectra[0].astype(jnp.float32)
    imag_part = spectra[1].astype(jnp.float32)
    powers = real_part * real_part + imag_part * imag_part
    smoother = smoothing(length_bins, HALF_BAND)
    counts = jnp.sum(smoother, axis=0)
    rows_flat = powers.reshape(-1, length_bins)
    smooth = jnp.dot(rows_flat, smoother, precision=lax.Precision.HIGHEST) / counts
    factor = lax.rsqrt(smooth + eps).reshape(powers.shape)
    return jnp.stack([real_part * factor, imag_part * factor]).astype(jnp.bfloat16)


def make_table(length_bins):
    bin_freq = np.float32(first_bin) + np.arange(length_bins, dtype=np.float32)
    lag_steps = np.arange(NLAG, dtype=np.float32) - np.float32(NLAG // 2)
    angles = np.float32(2.0 * math.pi / samples) * bin_freq[None, :] * lag_steps[:, None]
    return np.concatenate([np.cos(angles), -np.sin(angles)], axis=1).astype(ml_dtypes.bfloat16)


def arrange_kernel(x_ref, o_ref, turned):
    parts, channels, bins = x_ref.shape
    groups = bins // (QUADS * TILE)
    me = lax.rem(lax.axis_index("win"), QUADS)
    for part in range(parts):
        flipped = x_ref[part].astype(jnp.float32).T
        turned[part] = flipped.reshape(groups, QUADS, TILE, channels)

    def group_step(group, carry):
        rows = []
        for part in range(parts):
            for place in range(QUADS):
                quad = lax.rem(place - me + QUADS, QUADS)
                rows.append(turned[part, group, quad])
        o_ref[group] = jnp.concatenate(rows, axis=0).T.astype(o_ref.dtype)
        return carry

    lax.fori_loop(0, groups, group_step, 0, unroll=4)


def arrange(whitened):
    parts = whitened.shape[0] * whitened.shape[1]
    channels, bins = whitened.shape[2:]
    groups = bins // (QUADS * TILE)
    lanes = parts * QUADS * TILE
    return pl.pallas_call(
        arrange_kernel,
        out_shape=jax.ShapeDtypeStruct((groups, channels, lanes), jnp.bfloat16),
        in_specs=[pl.BlockSpec(memory_space=pltpu.VMEM)],
        out_specs=pl.BlockSpec(memory_space=pltpu.VMEM),
        scratch_shapes=[pltpu.VMEM((parts, groups, QUADS, TILE, channels), jnp.float32)],
        compiler_params=pltpu.CompilerParams(vmem_limit_bytes=24 * 2**20),
        name="arrange",
    )(whitened.reshape(parts, channels, bins))


def spread_kernel(reach, chans, wins, chunks, p_ref, o_ref, own_sem, s1, r1, s2, r2, s3, r3):
    chan = lax.axis_index("chan")
    win = lax.axis_index("win")
    row = win // CORES
    core = lax.rem(win, CORES)
    rows = wins // CORES
    other = row * CORES + (CORES - 1 - core)
    own = reach - 1
    size = p_ref.shape[0] // chunks
    offsets = list(range(1 - reach, reach + 1))
    order = sorted((o for o in offsets if o != 0), key=abs)

    def at(c):
        return lax.rem(c + chans, chans)

    def peer(step):
        return lax.rem(row + step + rows, rows) * CORES + core

    friends = sorted({o % chans for o in offsets if o} | {-o % chans for o in offsets if o})
    barrier = pltpu.get_barrier_semaphore()
    for f in friends:
        pl.semaphore_signal(barrier, inc=1, device_id=(at(chan + f), win), device_id_type=MESH)
    for step in range(1, rows):
        pl.semaphore_signal(barrier, inc=1, device_id=(chan, peer(step)), device_id_type=MESH)
    pl.semaphore_signal(barrier, inc=1, device_id=(chan, other), device_id_type=MESH)
    pl.semaphore_wait(barrier, len(friends) + rows)

    mine = pltpu.make_async_copy(p_ref, o_ref.at[own, win], own_sem)
    mine.start()

    def place(slot, piece, ch):
        return o_ref.at[slot, piece, pl.ds(ch * size, size)]

    def origin(slot, step, ch):
        if slot == own and step == 0:
            return p_ref.at[pl.ds(ch * size, size)]
        return place(slot, peer(-step), ch)

    def whole_way(o, ch):
        return abs(o) == 1 and ch % 2 == 0

    def along(o, step, ch):
        slot = o + own
        return pltpu.make_async_remote_copy(
            src_ref=origin(own, step, ch), dst_ref=place(slot, peer(-step), ch),
            send_sem=s1.at[slot, step, ch], recv_sem=r1.at[slot, step, ch],
            device_id=(at(chan - o), win), device_id_type=MESH)

    def across(slot, step, ch):
        return pltpu.make_async_remote_copy(
            src_ref=origin(slot, 0, ch), dst_ref=place(slot, win, ch),
            send_sem=s2.at[slot, step, ch], recv_sem=r2.at[slot, step, ch],
            device_id=(chan, peer(step)), device_id_type=MESH)

    def arrived(slot, step, ch):
        here = place(slot, peer(-step), ch)
        return pltpu.make_async_remote_copy(
            src_ref=here, dst_ref=here, send_sem=s2.at[slot, step, ch],
            recv_sem=r2.at[slot, step, ch], device_id=(chan, peer(step)), device_id_type=MESH)

    def beside(slot, step, ch):
        return pltpu.make_async_remote_copy(
            src_ref=origin(slot, step, ch), dst_ref=place(slot, peer(-step), ch),
            send_sem=s3.at[slot, step, ch], recv_sem=r3.at[slot, step, ch],
            device_id=(chan, other), device_id_type=MESH)

    def from_beside(slot, step, ch):
        base = lax.rem(row - step + rows, rows) * CORES + (CORES - 1 - core)
        here = place(slot, base, ch)
        return pltpu.make_async_remote_copy(
            src_ref=here, dst_ref=here, send_sem=s3.at[slot, step, ch],
            recv_sem=r3.at[slot, step, ch], device_id=(chan, other), device_id_type=MESH)

    steps = range(1, rows)
    for ch in range(chunks):
        for step in steps:
            across(own, step, ch).start()
        for o in order:
            along(o, 0, ch).start()
        beside(own, 0, ch).start()

    def second(ch):
        for step in steps:
            arrived(own, step, ch).wait_recv()
            for o in order:
                if whole_way(o, ch):
                    along(o, step, ch).start()
            beside(own, step, ch).start()
        for o in order:
            along(o, 0, ch).wait_recv()
            if not whole_way(o, ch):
                for step in steps:
                    across(o + own, step, ch).start()
            beside(o + own, 0, ch).start()

    def third(ch):
        for o in order:
            for step in steps:
                if whole_way(o, ch):
                    along(o, step, ch).wait_recv()
                else:
                    arrived(o + own, step, ch).wait_recv()
                beside(o + own, step, ch).start()

    for ch in range(chunks + 1):
        if ch < chunks:
            second(ch)
        if ch > 0:
            third(ch - 1)
    for ch in range(chunks):
        for o in offsets:
            for step in range(rows):
                from_beside(o + own, step, ch).wait_recv()
    for ch in range(chunks):
        for o in offsets:
            for step in range(rows):
                if o != 0 and (step == 0 or whole_way(o, ch)):
                    along(o, step, ch).wait_send()
                if step > 0 and (o == 0 or not whole_way(o, ch)):
                    across(o + own, step, ch).wait_send()
                beside(o + own, step, ch).wait_send()
    mine.wait()


def spread(piece, reach, chans, wins):
    slots = 2 * reach
    rows = wins // CORES
    chunks = 4 if rows <= 2 else 2
    sems = pltpu.SemaphoreType.DMA((slots, rows, chunks))
    return pl.pallas_call(
        functools.partial(spread_kernel, reach, chans, wins, chunks),
        out_shape=jax.ShapeDtypeStruct((slots, wins) + piece.shape, piece.dtype),
        in_specs=[pl.BlockSpec(memory_space=pl.ANY)],
        out_specs=pl.BlockSpec(memory_space=pl.ANY),
        scratch_shapes=[pltpu.SemaphoreType.DMA] + [sems] * 6,
        compiler_params=pltpu.CompilerParams(collective_id=0, has_side_effects=True),
        name="spread",
    )(piece)


def correlate_kernel(first_steps, scaling, pick_ref, a_ref, b_ref, t_ref, o_ref, cross):
    step = pl.program_id(0)
    wins, chunk, channels, lanes = a_ref.shape[1:]
    half = channels // 2
    bins = cross.shape[2]

    @pl.when(step < first_steps)
    def _():
        lane = lax.broadcasted_iota(jnp.int32, (1, lanes), 1)
        place = (lane // TILE) % QUADS
        keep = lax.broadcasted_iota(jnp.int32, (TILE, lanes), 0) == lax.broadcasted_iota(
            jnp.int32, (TILE, lanes), 1) % TILE
        keep = keep.astype(jnp.float32)[None]
        sign = jnp.where(lane < lanes // 2, -1.0, 1.0)
        zero = jnp.zeros((channels, lanes), jnp.bfloat16)

        def merged(ref, group, bundle, quad):
            out = ref[0, bundle * QUADS, group].astype(jnp.float32)
            for m in range(1, QUADS):
                part = ref[0, bundle * QUADS + m, group].astype(jnp.float32)
                out = jnp.where(place == (m + quad) % QUADS, part, out)
            return out

        def spread_rows(x):
            wide = jnp.broadcast_to(x[:, None, :], (half, TILE, lanes)) * keep
            return wide.reshape(half * TILE, lanes).astype(jnp.bfloat16)

        for group in range(chunk):
            for pair in range(QUADS // 2):
                both = []
                for quad in (2 * pair, 2 * pair + 1):
                    total = None
                    for bundle in range(wins // QUADS):
                        a = merged(a_ref, group, bundle, quad)
                        b = merged(b_ref, group, bundle, quad)
                        bx = (pltpu.roll(b, lanes // 2, 1) * sign).astype(jnp.bfloat16)
                        b = b.astype(jnp.bfloat16)
                        left = jnp.concatenate([spread_rows(a[:half]), spread_rows(a[half:])], axis=1)
                        right = jnp.concatenate(
                            [jnp.concatenate([b, zero, bx, zero], axis=0),
                             jnp.concatenate([zero, b, zero, bx], axis=0)], axis=1)
                        prod = lax.dot_general(left, right, (((1,), (1,)), ((), ())),
                                               preferred_element_type=jnp.float32)
                        total = prod if total is None else total + prod
                    both.append(total.reshape(half, TILE, 4 * channels))
                tile = jnp.concatenate(both, axis=1).astype(jnp.bfloat16)
                start = pl.multiple_of((step * chunk + group) * QUADS * TILE + pair * 2 * TILE, 2 * TILE)
                cross[0, :, pl.ds(start, 2 * TILE), :] = tile[:, :, :2 * channels]
                cross[1, :, pl.ds(start, 2 * TILE), :] = tile[:, :, 2 * channels:]

    @pl.when(step >= first_steps)
    def _():
        count = o_ref.shape[1]
        base = (step - first_steps) * count
        for p in range(0, count, 2):
            total = None
            for part in range(2):
                wide = jnp.concatenate([cross[part, base + p], cross[part, base + p + 1]], axis=1)
                prod = jnp.dot(t_ref[:, part * bins:(part + 1) * bins], wide,
                               preferred_element_type=jnp.float32)
                total = prod if total is None else total + prod
            turned = (total * scaling).T
            for q in range(2):
                for h in range(2):
                    begin = (2 * q + h) * channels
                    o_ref[h, p + q] = turned[begin:begin + channels]


def correlate(picks, nearby, table, scaling):
    slots, wins, groups, channels, lanes = nearby.shape
    bins = groups * QUADS * TILE
    half = channels // 2
    chunk = 2
    per_step = 4
    first_steps = groups // chunk
    last_steps = half // per_step

    def source(which):
        return lambda s, pick: (pick[which], 0, jnp.minimum(s, first_steps - 1), 0, 0)

    block = (1, wins, chunk, channels, lanes)
    out = pl.pallas_call(
        functools.partial(correlate_kernel, first_steps, scaling),
        out_shape=jax.ShapeDtypeStruct((2, half, channels, NLAG), jnp.float32),
        grid_spec=pltpu.PrefetchScalarGridSpec(
            num_scalar_prefetch=1,
            grid=(first_steps + last_steps,),
            in_specs=[
                pl.BlockSpec(block, source(0)),
                pl.BlockSpec(block, source(1)),
                pl.BlockSpec((NLAG, 2 * bins), lambda s, pick: (0, 0)),
            ],
            out_specs=pl.BlockSpec(
                (2, per_step, channels, NLAG),
                lambda s, pick: (0, jnp.maximum(s - first_steps, 0), 0, 0)),
            scratch_shapes=[pltpu.VMEM((2, half, bins, 2 * channels), jnp.bfloat16)],
        ),
        compiler_params=pltpu.CompilerParams(
            dimension_semantics=("arbitrary",), vmem_limit_bytes=48 * 2**20),
        name="correlate",
    )(picks, nearby, nearby, table)
    return out.reshape(channels, channels, NLAG)


def per_device(chans, wins, spectra, pair_blocks):
    whitened = whiten(spectra)
    length_bins = spectra.shape[3]
    reach = pair_blocks.shape[0] * wins // 2
    table = jnp.asarray(make_table(length_bins))
    scaling = 1.0 / math.sqrt(spectra.shape[1] * wins * length_bins)
    base_block = lax.axis_index("chan") - (reach - 1)
    picks = jnp.mod(pair_blocks - base_block, chans)
    nearby = spread(arrange(whitened), reach, chans, wins)
    rows = [correlate(picks[r], nearby, table, scaling) for r in range(pair_blocks.shape[0])]
    return jnp.stack(rows)


def solution(mesh):
    in_specs = (P(None, "win", "chan", None), P(("chan", "win"), None))
    out_specs = P(("chan", "win"), None, None, None)
    return jax.shard_map(
        functools.partial(per_device, mesh.shape["chan"], mesh.shape["win"]),
        mesh=mesh, in_specs=in_specs, out_specs=out_specs, check_vma=False
    )
```

profile of v0, /device:TPU:0, one launch (start us, length us, event | category | flops | bytes accessed | tf_op | source)
XLA Modules:
  0.0 79.5 jit_solution(7142501075553201197)
XLA Ops:
  0.0 0.0 copy-start.2
  0.0 0.7 fusion.8.pick_ref
  0.7 0.2 convert_reduce_fusion
  0.9 1.1 %fusion.5 = f32[1,2,64,1024]{3,2,1,0:T(8,128)S(1)} fusion(bf16[2,2,64,1024]{3,2,1,0:T(8,128)(2,1)} %param.3), kind=kLoop, calls=%fused_computation.11 | loop fusion | flops 655360 | bytes 1048576 | tf_op jit(solution)/shard_map/add | solution.py:35
  2.1 1.1 %fusion.4 = f32[128,1024]{1,0:T(8,128)S(1)} fusion(f32[128,1024]{1,0:T(8,128)S(1)} %bitcast.9, f32[1024]{0:T(1024)S(1)} %convert_reduce_fusion), kind=kOutput, calls=%fused_computation.6 | convolution fusion | flops 1614020608 | bytes 1052672 | tf_op jit(solution)/shard_map/dot_general | solution.py:39
  3.2 0.0 copy-done.2
  3.2 0.1 fusion.6
  3.3 0.1 pad_maximum_fusion
  3.4 1.1 %arrange.1.p_ref = bf16[32,64,128]{2,1,0:T(8,128)(2,1)S(1)} custom-call(bf16[4,64,1024]{2,1,0:T(8,128)(2,1)S(1)} %bitcast.7), custom_call_target="tpu_custom_call" | custom-call | tf_op jit(solution)/shard_map/arrange/pallas_call | solution.py:76
  4.4 0.0 copy-start
  4.4 0.8 copy-done
  5.2 0.0 copy-start.1
  5.2 52.0 %spread.1.a_ref.b_ref = bf16[4,4,32,64,128]{4,3,2,1,0:T(8,128)(2,1)} custom-call(bf16[32,64,128]{2,1,0:T(8,128)(2,1)} %copy-done), custom_call_target="tpu_custom_call" | custom-call | tf_op jit(solution)/shard_map/spread/pallas_call | solution.py:216
  57.2 0.0 copy-done.1
  57.2 22.3 %correlate.1 = f32[2,32,64,256]{3,2,1,0:T(8,128)} custom-call(s32[2]{0:T(128)S(1)} %fusion.8.pick_ref, bf16[4,4,32,64,128]{4,3,2,1,0:T(8,128)(2,1)} %spread.1.a_ref.b_ref, bf16[4,4,32,64,128]{4,3,2,1,0:T(8,128)(2,1)} %spread.1.a_ref.b_ref, bf16[256,2048]{1,0:T(8,128)(2,1)S(1)} %copy-done.1), custom_call_target="tpu_custom_call" | custom-call | tf_op jit(solution)/shard_map/correlate/pallas_call | solution.py:308
Async XLA Ops:
  0.0 3.2 %copy-start.2 = (bf16[2,2,64,1024]{3,2,1,0:T(8,128)(2,1)S(1)}, bf16[2,2,64,1024]{3,2,1,0:T(8,128)(2,1)}, u32[]{:S(2)}) copy-start(bf16[2,2,64,1024]{3,2,1,0:T(8,128)(2,1)} %param.3) | copy-start | bytes 1572868
  4.4 0.8 %copy-start = (bf16[32,64,128]{2,1,0:T(8,128)(2,1)}, bf16[32,64,128]{2,1,0:T(8,128)(2,1)S(1)}, u32[]{:S(2)}) copy-start(bf16[32,64,128]{2,1,0:T(8,128)(2,1)S(1)} %arrange.1.p_ref) | copy-start | bytes 1572868
  5.2 52.0 %copy-start.1 = (bf16[256,2048]{1,0:T(8,128)(2,1)S(1)}, bf16[256,2048]{1,0:T(8,128)(2,1)}, u32[]{:S(2)}) copy-start(bf16[256,2048]{1,0:T(8,128)(2,1)} %constant.32.clone.t_ref) | copy-start | bytes 3145732
where the time goes:
time: 80 us; the launch traced here: 79.5 us
  Pallas kernels  75.3 us (94%)
  other arithmetic  2.24 us (3%)
  matrix products  1.09 us (1%)
  local copies, waits for them, and re-layouts  0.8 us (1%)
    pallas_call x1, Pallas kernels, spread(): pl.pallas_call(functools.partial(spread_kernel, reach, chans, wins, chunk...  52 us
    pallas_call x1, Pallas kernels, correlate(): pl.pallas_call(functools.partial(correlate_kernel, first_steps, scaling),...  22.3 us

commit v1 on v0

--- a/solution.py
+++ b/solution.py
@@ -84,7 +84,76 @@
     )(whitened.reshape(parts, channels, bins))
 
 
-def spread_kernel(reach, chans, wins, chunks, p_ref, o_ref, own_sem, s1, r1, s2, r2, s3, r3):
+def cross_chunk(pick, buf, cross):
+    _, wins, groups, channels, lanes = buf.shape
+    half = channels // 2
+    lane = lax.broadcasted_iota(jnp.int32, (1, lanes), 1)
+    place = (lane // TILE) % QUADS
+    keep = lax.broadcasted_iota(jnp.int32, (TILE, lanes), 0) == lax.broadcasted_iota(
+        jnp.int32, (TILE, lanes), 1) % TILE
+    keep = keep.astype(jnp.float32)[None]
+    sign = jnp.where(lane < lanes // 2, -1.0, 1.0)
+    zero = jnp.zeros((channels, lanes), jnp.bfloat16)
+
+    def merged(pieces, quad):
+        out = pieces[0]
+        for m in range(1, QUADS):
+            out = jnp.where(place == (m + quad) % QUADS, pieces[m], out)
+        return out
+
+    def spread_rows(x):
+        wide = jnp.broadcast_to(x[:, None, :], (half, TILE, lanes)) * keep
+        return wide.reshape(half * TILE, lanes).astype(jnp.bfloat16)
+
+    def group_step(group, carry):
+        a_pieces = [buf[pick[0], m, group].astype(jnp.float32) for m in range(wins)]
+        b_pieces = [buf[pick[1], m, group].astype(jnp.float32) for m in range(wins)]
+        for pair in range(QUADS // 2):
+            both = []
+            for quad in (2 * pair, 2 * pair + 1):
+                total = None
+                for bundle in range(0, wins, QUADS):
+                    a = merged(a_pieces[bundle:bundle + QUADS], quad)
+                    b = merged(b_pieces[bundle:bundle + QUADS], quad)
+                    bx = (pltpu.roll(b, lanes // 2, 1) * sign).astype(jnp.bfloat16)
+                    b = b.astype(jnp.bfloat16)
+                    left = jnp.concatenate([spread_rows(a[:half]), spread_rows(a[half:])], axis=1)
+                    right = jnp.concatenate(
+                        [jnp.concatenate([b, zero, bx, zero], axis=0),
+                         jnp.concatenate([zero, b, zero, bx], axis=0)], axis=1)
+                    prod = lax.dot_general(left, right, (((1,), (1,)), ((), ())),
+                                           preferred_element_type=jnp.float32)
+                    total = prod if total is None else total + prod
+                both.append(total.reshape(half, TILE, 4 * channels))
+            tile = jnp.concatenate(both, axis=1).astype(jnp.bfloat16)
+            start = pl.multiple_of(group * (QUADS * TILE) + pair * 2 * TILE, 2 * TILE)
+            cross[0, :, pl.ds(start, 2 * TILE), :] = tile[:, :, :2 * channels]
+            cross[1, :, pl.ds(start, 2 * TILE), :] = tile[:, :, 2 * channels:]
+        return carry
+
+    lax.fori_loop(0, groups, group_step, 0, unroll=2)
+
+
+def lag_chunk(begin, bins, t_ref, cross, o_ref):
+    size = cross.shape[2]
+
+    def pair_step(p, carry):
+        total = None
+        for part in range(2):
+            wide = jnp.concatenate([cross[part, 2 * p], cross[part, 2 * p + 1]], axis=1)
+            first = part * bins + begin
+            prod = jnp.dot(t_ref[:, first:first + size], wide, preferred_element_type=jnp.float32)
+            total = prod if total is None else total + prod
+        if begin:
+            total = total + o_ref[p]
+        o_ref[p] = total
+        return carry
+
+    lax.fori_loop(0, o_ref.shape[0], pair_step, 0, unroll=2)
+
+
+def spread_kernel(reach, chans, wins, chunks, pair_ref, p_ref, t_ref, o_ref, cross, own_sem,
+                  s1, r1, s2, r2, s3, r3, *bufs):
     chan = lax.axis_index("chan")
     win = lax.axis_index("win")
     row = win // CORES
@@ -111,11 +180,11 @@
     pl.semaphore_signal(barrier, inc=1, device_id=(chan, other), device_id_type=MESH)
     pl.semaphore_wait(barrier, len(friends) + rows)
 
-    mine = pltpu.make_async_copy(p_ref, o_ref.at[own, win], own_sem)
-    mine.start()
+    def mine(ch):
+        return pltpu.make_async_copy(origin(own, 0, ch), place(own, win, ch), own_sem.at[ch])
 
     def place(slot, piece, ch):
-        return o_ref.at[slot, piece, pl.ds(ch * size, size)]
+        return bufs[ch].at[slot, piece]
 
     def origin(slot, step, ch):
         if slot == own and step == 0:
@@ -164,6 +233,7 @@
         for o in order:
             along(o, 0, ch).start()
         beside(own, 0, ch).start()
+        mine(ch).start()
 
     def second(ch):
         for step in steps:
@@ -188,15 +258,25 @@
                     arrived(o + own, step, ch).wait_recv()
                 beside(o + own, step, ch).start()
 
-    for ch in range(chunks + 1):
-        if ch < chunks:
-            second(ch)
-        if ch > 0:
-            third(ch - 1)
-    for ch in range(chunks):
+    pick = [jnp.minimum(lax.rem(pair_ref[0, n] - (chan - own) + 2 * chans, chans), 2 * reach - 1)
+            for n in range(2)]
+    bins = t_ref.shape[1] // 2
+
+    def compute(ch):
+        mine(ch).wait()
         for o in offsets:
             for step in range(rows):
                 from_beside(o + own, step, ch).wait_recv()
+        cross_chunk(pick, bufs[ch], cross)
+        lag_chunk(ch * (bins // chunks), bins, t_ref, cross, o_ref)
+
+    for ch in range(chunks + 2):
+        if ch < chunks:
+            second(ch)
+        if 0 <= ch - 1 < chunks:
+            third(ch - 1)
+        if ch - 2 >= 0:
+            compute(ch - 2)
     for ch in range(chunks):
         for o in offsets:
             for step in range(rows):
@@ -205,127 +285,56 @@
                 if step > 0 and (o == 0 or not whole_way(o, ch)):
                     across(o + own, step, ch).wait_send()
                 beside(o + own, step, ch).wait_send()
-    mine.wait()
-
-
-def spread(piece, reach, chans, wins):
+
+
+def spread(pairs, piece, table, reach, chans, wins):
     slots = 2 * reach
     rows = wins // CORES
-    chunks = 4 if rows <= 2 else 2
+    chunks = 4
+    groups, channels, lanes = piece.shape
+    lags, bins = table.shape[0], table.shape[1] // 2
+    half = channels // 2
+    size = groups // chunks
     sems = pltpu.SemaphoreType.DMA((slots, rows, chunks))
+    buf = pltpu.VMEM((slots, wins, size, channels, lanes), piece.dtype)
+    vmem = pl.BlockSpec(memory_space=pltpu.VMEM)
     return pl.pallas_call(
         functools.partial(spread_kernel, reach, chans, wins, chunks),
-        out_shape=jax.ShapeDtypeStruct((slots, wins) + piece.shape, piece.dtype),
-        in_specs=[pl.BlockSpec(memory_space=pl.ANY)],
-        out_specs=pl.BlockSpec(memory_space=pl.ANY),
-        scratch_shapes=[pltpu.SemaphoreType.DMA] + [sems] * 6,
-        compiler_params=pltpu.CompilerParams(collective_id=0, has_side_effects=True),
+        out_shape=jax.ShapeDtypeStruct((half // 2, lags, 4 * channels), jnp.float32),
+        in_specs=[pl.BlockSpec(memory_space=pltpu.SMEM), vmem, vmem],
+        out_specs=vmem,
+        scratch_shapes=[pltpu.VMEM((2, half, bins // chunks, 2 * channels), jnp.bfloat16),
+                        pltpu.SemaphoreType.DMA((chunks,))] + [sems] * 6 + [buf] * chunks,
+        compiler_params=pltpu.CompilerParams(
+            collective_id=0, has_side_effects=True, vmem_limit_bytes=56 * 2**20),
         name="spread",
-    )(piece)
-
-
-def correlate_kernel(first_steps, scaling, pick_ref, a_ref, b_ref, t_ref, o_ref, cross):
-    step = pl.program_id(0)
-    wins, chunk, channels, lanes = a_ref.shape[1:]
-    half = channels // 2
-    bins = cross.shape[2]
-
-    @pl.when(step < first_steps)
-    def _():
-        lane = lax.broadcasted_iota(jnp.int32, (1, lanes), 1)
-        place = (lane // TILE) % QUADS
-        keep = lax.broadcasted_iota(jnp.int32, (TILE, lanes), 0) == lax.broadcasted_iota(
-            jnp.int32, (TILE, lanes), 1) % TILE
-        keep = keep.astype(jnp.float32)[None]
-        sign = jnp.where(lane < lanes // 2, -1.0, 1.0)
-        zero = jnp.zeros((channels, lanes), jnp.bfloat16)
-
-        def merged(ref, group, bundle, quad):
-            out = ref[0, bundle * QUADS, group].astype(jnp.float32)
-            for m in range(1, QUADS):
-                part = ref[0, bundle * QUADS + m, group].astype(jnp.float32)
-                out = jnp.where(place == (m + quad) % QUADS, part, out)
-            return out
-
-        def spread_rows(x):
-            wide = jnp.broadcast_to(x[:, None, :], (half, TILE, lanes)) * keep
-            return wide.reshape(half * TILE, lanes).astype(jnp.bfloat16)
-
-        for group in range(chunk):
-            for pair in range(QUADS // 2):
-                both = []
-                for quad in (2 * pair, 2 * pair + 1):
-                    total = None
-                    for bundle in range(wins // QUADS):
-                        a = merged(a_ref, group, bundle, quad)
-                        b = merged(b_ref, group, bundle, quad)
-                        bx = (pltpu.roll(b, lanes // 2, 1) * sign).astype(jnp.bfloat16)
-                        b = b.astype(jnp.bfloat16)
-                        left = jnp.concatenate([spread_rows(a[:half]), spread_rows(a[half:])], axis=1)
-                        right = jnp.concatenate(
-                            [jnp.concatenate([b, zero, bx, zero], axis=0),
-                             jnp.concatenate([zero, b, zero, bx], axis=0)], axis=1)
-                        prod = lax.dot_general(left, right, (((1,), (1,)), ((), ())),
-                                               preferred_element_type=jnp.float32)
-                        total = prod if total is None else total + prod
-                    both.append(total.reshape(half, TILE, 4 * channels))
-                tile = jnp.concatenate(both, axis=1).astype(jnp.bfloat16)
-                start = pl.multiple_of((step * chunk + group) * QUADS * TILE + pair * 2 * TILE, 2 * TILE)
-                cross[0, :, pl.ds(start, 2 * TILE), :] = tile[:, :, :2 * channels]
-                cross[1, :, pl.ds(start, 2 * TILE), :] = tile[:, :, 2 * channels:]
-
-    @pl.when(step >= first_steps)
-    def _():
-        count = o_ref.shape[1]
-        base = (step - first_steps) * count
-        for p in range(0, count, 2):
-            total = None
-            for part in range(2):
-                wide = jnp.concatenate([cross[part, base + p], cross[part, base + p + 1]], axis=1)
-                prod = jnp.dot(t_ref[:, part * bins:(part + 1) * bins], wide,
-                               preferred_element_type=jnp.float32)
-                total = prod if total is None else total + prod
-            turned = (total * scaling).T
-            for q in range(2):
-                for h in range(2):
-                    begin = (2 * q + h) * channels
-                    o_ref[h, p + q] = turned[begin:begin + channels]
-
-
-def correlate(picks, nearby, table, scaling):
-    slots, wins, groups, channels, lanes = nearby.shape
-    bins = groups * QUADS * TILE
-    half = channels // 2
-    chunk = 2
-    per_step = 4
-    first_steps = groups // chunk
-    last_steps = half // per_step
-
-    def source(which):
-        return lambda s, pick: (pick[which], 0, jnp.minimum(s, first_steps - 1), 0, 0)
-
-    block = (1, wins, chunk, channels, lanes)
+    )(pairs, piece, table)
+
+
+def finish_kernel(scaling, x_ref, o_ref):
+    channels = o_ref.shape[2]
+    for p in range(x_ref.shape[0]):
+        turned = (x_ref[p] * scaling).T
+        for q in range(2):
+            for h in range(2):
+                begin = (2 * q + h) * channels
+                o_ref[h, 2 * p + q] = turned[begin:begin + channels]
+
+
+def finish(sums, scaling):
+    count, lags, width = sums.shape
+    channels = width // 4
+    per_step = 2
     out = pl.pallas_call(
-        functools.partial(correlate_kernel, first_steps, scaling),
-        out_shape=jax.ShapeDtypeStruct((2, half, channels, NLAG), jnp.float32),
-        grid_spec=pltpu.PrefetchScalarGridSpec(
-            num_scalar_prefetch=1,
-            grid=(first_steps + last_steps,),
-            in_specs=[
-                pl.BlockSpec(block, source(0)),
-                pl.BlockSpec(block, source(1)),
-                pl.BlockSpec((NLAG, 2 * bins), lambda s, pick: (0, 0)),
-            ],
-            out_specs=pl.BlockSpec(
-                (2, per_step, channels, NLAG),
-                lambda s, pick: (0, jnp.maximum(s - first_steps, 0), 0, 0)),
-            scratch_shapes=[pltpu.VMEM((2, half, bins, 2 * channels), jnp.bfloat16)],
-        ),
-        compiler_params=pltpu.CompilerParams(
-            dimension_semantics=("arbitrary",), vmem_limit_bytes=48 * 2**20),
-        name="correlate",
-    )(picks, nearby, nearby, table)
-    return out.reshape(channels, channels, NLAG)
+        functools.partial(finish_kernel, scaling),
+        out_shape=jax.ShapeDtypeStruct((2, 2 * count, channels, lags), jnp.float32),
+        grid=(count // per_step,),
+        in_specs=[pl.BlockSpec((per_step, lags, width), lambda s: (s, 0, 0))],
+        out_specs=pl.BlockSpec((2, 2 * per_step, channels, lags), lambda s: (0, s, 0, 0)),
+        compiler_params=pltpu.CompilerParams(vmem_limit_bytes=24 * 2**20),
+        name="finish",
+    )(sums)
+    return out.reshape(1, channels, channels, lags)
 
 
 def per_device(chans, wins, spectra, pair_blocks):
@@ -334,11 +343,7 @@
     reach = pair_blocks.shape[0] * wins // 2
     table = jnp.asarray(make_table(length_bins))
     scaling = 1.0 / math.sqrt(spectra.shape[1] * wins * length_bins)
-    base_block = lax.axis_index("chan") - (reach - 1)
-    picks = jnp.mod(pair_blocks - base_block, chans)
-    nearby = spread(arrange(whitened), reach, chans, wins)
-    rows = [correlate(picks[r], nearby, table, scaling) for r in range(pair_blocks.shape[0])]
-    return jnp.stack(rows)
+    return finish(spread(pair_blocks, arrange(whitened), table, reach, chans, wins), scaling)
 
 
 def solution(mesh):

time: 80 us -> 77.3 us (0.966)
  Pallas kernels: 75.3 us -> 71.5 us
  local copies, waits for them, and re-layouts: 0.8 us -> 2.97 us
    pallas_call x1, Pallas kernels: 22.3 us -> 4.19 us  [finish(): pl.pallas_call(functools.partial(finish_kernel, scaling), out_shape=jax.S...]
    pallas_call x1, Pallas kernels: 52 us -> 66.2 us  [spread(): pl.pallas_call(functools.partial(spread_kernel, reach, chans, wins, chunk...]
    unnamed x6, local copies, waits for them, and re-layouts: 0.8 us -> 2.97 us
where the time goes in v1:
time: 77.3 us; the launch traced here: 77.1 us
  Pallas kernels  71.5 us (92%)
  local copies, waits for them, and re-layouts  2.97 us (4%)
  other arithmetic  1.52 us (2%)
  matrix products  1.09 us (1%)
    pallas_call x1, Pallas kernels, spread(): pl.pallas_call(functools.partial(spread_kernel, reach, chans, wins, chunk...  66.2 us
    pallas_call x1, Pallas kernels, finish(): pl.pallas_call(functools.partial(finish_kernel, scaling), out_shape=jax.S...  4.19 us
    unnamed x6, local copies, waits for them, and re-layouts  2.97 us

profile of v1, /device:TPU:0, one launch (start us, length us, event | category | flops | bytes accessed | tf_op | source)
XLA Modules:
  0.0 77.1 jit_solution(758132888617348706)
XLA Ops:
  0.0 0.0 copy-start.2
  0.0 0.2 convert_reduce_fusion
  0.2 1.1 %fusion.5 = f32[1,2,64,1024]{3,2,1,0:T(8,128)S(1)} fusion(bf16[2,2,64,1024]{3,2,1,0:T(8,128)(2,1)} %param.3), kind=kLoop, calls=%fused_computation.11 | loop fusion | flops 655360 | bytes 1048576 | tf_op jit(solution)/shard_map/add | solution.py:35
  1.3 1.1 %fusion.4 = f32[128,1024]{1,0:T(8,128)S(1)} fusion(f32[128,1024]{1,0:T(8,128)S(1)} %bitcast.7, f32[1024]{0:T(1024)S(1)} %convert_reduce_fusion), kind=kOutput, calls=%fused_computation.6 | convolution fusion | flops 1614020608 | bytes 1052672 | tf_op jit(solution)/shard_map/dot_general | solution.py:39
  2.4 0.0 copy-done.2
  2.5 0.1 fusion.6
  2.6 0.1 pad_maximum_fusion
  2.7 1.1 %arrange.1.p_ref = bf16[32,64,128]{2,1,0:T(8,128)(2,1)S(1)} custom-call(bf16[4,64,1024]{2,1,0:T(8,128)(2,1)S(1)} %bitcast.5), custom_call_target="tpu_custom_call" | custom-call | tf_op jit(solution)/shard_map/arrange/pallas_call | solution.py:76
  3.7 0.0 copy-start.1
  3.7 0.8 %copy-done.1 = bf16[32,64,128]{2,1,0:T(8,128)(2,1)} copy-done((bf16[32,64,128]{2,1,0:T(8,128)(2,1)}, bf16[32,64,128]{2,1,0:T(8,128)(2,1)S(1)}, u32[]{:S(2)}) %copy-start.1) | copy-done | bytes 524312
  4.5 66.2 %spread.1.x_ref = f32[16,256,256]{2,1,0:T(8,128)} custom-call(s32[1,2]{1,0:T(1,128)} %pair_ref.1, bf16[32,64,128]{2,1,0:T(8,128)(2,1)} %copy-done.1, bf16[256,2048]{1,0:T(8,128)(2,1)} %constant.8.clone.t_ref), custom_call_target="tpu_custom_call" | custom-call | tf_op jit(solution)/shard_map/spread/pallas_call | solution.py:301
  70.7 0.0 copy-start
  70.7 2.2 %copy-done = f32[16,256,256]{2,1,0:T(8,128)S(1)} copy-done((f32[16,256,256]{2,1,0:T(8,128)S(1)}, f32[16,256,256]{2,1,0:T(8,128)}, u32[]{:S(2)}) %copy-start) | copy-done | bytes 4194328
  72.9 4.2 %finish.1 = f32[2,32,64,256]{3,2,1,0:T(8,128)} custom-call(f32[16,256,256]{2,1,0:T(8,128)S(1)} %copy-done), custom_call_target="tpu_custom_call" | custom-call | tf_op jit(solution)/shard_map/finish/pallas_call | solution.py:328
Async XLA Ops:
  0.0 2.4 %copy-start.2 = (bf16[2,2,64,1024]{3,2,1,0:T(8,128)(2,1)S(1)}, bf16[2,2,64,1024]{3,2,1,0:T(8,128)(2,1)}, u32[]{:S(2)}) copy-start(bf16[2,2,64,1024]{3,2,1,0:T(8,128)(2,1)} %param.3) | copy-start | bytes 1572868
  3.7 0.8 %copy-start.1 = (bf16[32,64,128]{2,1,0:T(8,128)(2,1)}, bf16[32,64,128]{2,1,0:T(8,128)(2,1)S(1)}, u32[]{:S(2)}) copy-start(bf16[32,64,128]{2,1,0:T(8,128)(2,1)S(1)} %arrange.1.p_ref) | copy-start | bytes 1572868
  70.7 2.2 %copy-start = (f32[16,256,256]{2,1,0:T(8,128)S(1)}, f32[16,256,256]{2,1,0:T(8,128)}, u32[]{:S(2)}) copy-start(f32[16,256,256]{2,1,0:T(8,128)} %spread.1.x_ref) | copy-start | bytes 12582916

commit v2 on v1

--- a/solution.py
+++ b/solution.py
@@ -89,9 +89,9 @@
     half = channels // 2
     lane = lax.broadcasted_iota(jnp.int32, (1, lanes), 1)
     place = (lane // TILE) % QUADS
-    keep = lax.broadcasted_iota(jnp.int32, (TILE, lanes), 0) == lax.broadcasted_iota(
-        jnp.int32, (TILE, lanes), 1) % TILE
-    keep = keep.astype(jnp.float32)[None]
+    keep = lax.broadcasted_iota(jnp.int32, (2 * TILE, lanes), 0) % TILE == lax.broadcasted_iota(
+        jnp.int32, (2 * TILE, lanes), 1) % TILE
+    keep = keep.astype(jnp.float32).astype(jnp.bfloat16)[None]
     sign = jnp.where(lane < lanes // 2, -1.0, 1.0)
     zero = jnp.zeros((channels, lanes), jnp.bfloat16)
 
@@ -102,8 +102,9 @@
         return out
 
     def spread_rows(x):
-        wide = jnp.broadcast_to(x[:, None, :], (half, TILE, lanes)) * keep
-        return wide.reshape(half * TILE, lanes).astype(jnp.bfloat16)
+        wide = jnp.broadcast_to(x[:, None, :], (half, TILE, lanes))
+        wide = wide.reshape(half * TILE // (2 * TILE), 2 * TILE, lanes).astype(jnp.bfloat16) * keep
+        return wide.reshape(half * TILE, lanes)
 
     def group_step(group, carry):
         a_pieces = [buf[pick[0], m, group].astype(jnp.float32) for m in range(wins)]
@@ -127,33 +128,37 @@
                 both.append(total.reshape(half, TILE, 4 * channels))
             tile = jnp.concatenate(both, axis=1).astype(jnp.bfloat16)
             start = pl.multiple_of(group * (QUADS * TILE) + pair * 2 * TILE, 2 * TILE)
-            cross[0, :, pl.ds(start, 2 * TILE), :] = tile[:, :, :2 * channels]
-            cross[1, :, pl.ds(start, 2 * TILE), :] = tile[:, :, 2 * channels:]
+            cross[:, 0, pl.ds(start, 2 * TILE), :] = tile[:, :, :2 * channels]
+            cross[:, 1, pl.ds(start, 2 * TILE), :] = tile[:, :, 2 * channels:]
         return carry
 
     lax.fori_loop(0, groups, group_step, 0, unroll=2)
 
 
-def lag_chunk(begin, bins, t_ref, cross, o_ref):
-    size = cross.shape[2]
+def lag_chunk(ch, chunks, scaling, t_ref, cross, sums, send):
+    count, quarters, channels, width = sums.shape
+    size = 2 * cross.shape[2]
 
     def pair_step(p, carry):
-        total = None
-        for part in range(2):
-            wide = jnp.concatenate([cross[part, 2 * p], cross[part, 2 * p + 1]], axis=1)
-            first = part * bins + begin
-            prod = jnp.dot(t_ref[:, first:first + size], wide, preferred_element_type=jnp.float32)
-            total = prod if total is None else total + prod
-        if begin:
-            total = total + o_ref[p]
-        o_ref[p] = total
+        wide = jnp.concatenate([cross[2 * p].reshape(size, width // 2),
+                                cross[2 * p + 1].reshape(size, width // 2)], axis=1)
+        total = jnp.dot(t_ref[:, ch * size:(ch + 1) * size], wide,
+                        preferred_element_type=jnp.float32)
+        if ch:
+            total = total + sums[p].reshape(quarters * channels, width)
+        if ch == chunks - 1:
+            total = (total * scaling).T
+        sums[p] = total.reshape(quarters, channels, width)
+        if ch == chunks - 1:
+            for n in range(quarters):
+                send(p, n).start()
         return carry
 
-    lax.fori_loop(0, o_ref.shape[0], pair_step, 0, unroll=2)
-
-
-def spread_kernel(reach, chans, wins, chunks, pair_ref, p_ref, t_ref, o_ref, cross, own_sem,
-                  s1, r1, s2, r2, s3, r3, *bufs):
+    lax.fori_loop(0, count, pair_step, 0, unroll=2)
+
+
+def spread_kernel(reach, chans, wins, chunks, scaling, pair_ref, p_ref, t_ref, o_ref, cross, sums,
+                  out_sem, own_sem, s1, r1, s2, r2, s3, r3, *bufs):
     chan = lax.axis_index("chan")
     win = lax.axis_index("win")
     row = win // CORES
@@ -227,13 +232,18 @@
             recv_sem=r3.at[slot, step, ch], device_id=(chan, other), device_id_type=MESH)
 
     steps = range(1, rows)
-    for ch in range(chunks):
+
+    def begin(ch):
         for step in steps:
             across(own, step, ch).start()
         for o in order:
             along(o, 0, ch).start()
         beside(own, 0, ch).start()
         mine(ch).start()
+
+    def send(p, n):
+        return pltpu.make_async_copy(
+            sums.at[p, n], o_ref.at[n % 2, 2 * p + n // 2], out_sem.at[p, n])
 
     def second(ch):
         for step in steps:
@@ -260,7 +270,6 @@
 
     pick = [jnp.minimum(lax.rem(pair_ref[0, n] - (chan - own) + 2 * chans, chans), 2 * reach - 1)
             for n in range(2)]
-    bins = t_ref.shape[1] // 2
 
     def compute(ch):
         mine(ch).wait()
@@ -268,11 +277,15 @@
             for step in range(rows):
                 from_beside(o + own, step, ch).wait_recv()
         cross_chunk(pick, bufs[ch], cross)
-        lag_chunk(ch * (bins // chunks), bins, t_ref, cross, o_ref)
-
+        lag_chunk(ch, chunks, scaling, t_ref, cross, sums, send)
+
+    begin(0)
+    begin(1)
     for ch in range(chunks + 2):
         if ch < chunks:
             second(ch)
+        if ch + 2 < chunks:
+            begin(ch + 2)
         if 0 <= ch - 1 < chunks:
             third(ch - 1)
         if ch - 2 >= 0:
@@ -286,11 +299,17 @@
                     across(o + own, step, ch).wait_send()
                 beside(o + own, step, ch).wait_send()
 
-
-def spread(pairs, piece, table, reach, chans, wins):
+    def drain(p, carry):
+        for n in range(sums.shape[1]):
+            send(p, n).wait()
+        return carry
+
+    lax.fori_loop(0, sums.shape[0], drain, 0)
+
+
+def spread(pairs, piece, table, scaling, reach, chans, wins, chunks):
     slots = 2 * reach
     rows = wins // CORES
-    chunks = 4
     groups, channels, lanes = piece.shape
     lags, bins = table.shape[0], table.shape[1] // 2
     half = channels // 2
@@ -298,42 +317,19 @@
     sems = pltpu.SemaphoreType.DMA((slots, rows, chunks))
     buf = pltpu.VMEM((slots, wins, size, channels, lanes), piece.dtype)
     vmem = pl.BlockSpec(memory_space=pltpu.VMEM)
-    return pl.pallas_call(
-        functools.partial(spread_kernel, reach, chans, wins, chunks),
-        out_shape=jax.ShapeDtypeStruct((half // 2, lags, 4 * channels), jnp.float32),
+    out = pl.pallas_call(
+        functools.partial(spread_kernel, reach, chans, wins, chunks, scaling),
+        out_shape=jax.ShapeDtypeStruct((2, half, channels, lags), jnp.float32),
         in_specs=[pl.BlockSpec(memory_space=pltpu.SMEM), vmem, vmem],
-        out_specs=vmem,
-        scratch_shapes=[pltpu.VMEM((2, half, bins // chunks, 2 * channels), jnp.bfloat16),
+        out_specs=pl.BlockSpec(memory_space=pl.ANY),
+        scratch_shapes=[pltpu.VMEM((half, 2, bins // chunks, 2 * channels), jnp.bfloat16),
+                        pltpu.VMEM((half // 2, 4, channels, lags), jnp.float32),
+                        pltpu.SemaphoreType.DMA((half // 2, 4)),
                         pltpu.SemaphoreType.DMA((chunks,))] + [sems] * 6 + [buf] * chunks,
         compiler_params=pltpu.CompilerParams(
             collective_id=0, has_side_effects=True, vmem_limit_bytes=56 * 2**20),
         name="spread",
     )(pairs, piece, table)
-
-
-def finish_kernel(scaling, x_ref, o_ref):
-    channels = o_ref.shape[2]
-    for p in range(x_ref.shape[0]):
-        turned = (x_ref[p] * scaling).T
-        for q in range(2):
-            for h in range(2):
-                begin = (2 * q + h) * channels
-                o_ref[h, 2 * p + q] = turned[begin:begin + channels]
-
-
-def finish(sums, scaling):
-    count, lags, width = sums.shape
-    channels = width // 4
-    per_step = 2
-    out = pl.pallas_call(
-        functools.partial(finish_kernel, scaling),
-        out_shape=jax.ShapeDtypeStruct((2, 2 * count, channels, lags), jnp.float32),
-        grid=(count // per_step,),
-        in_specs=[pl.BlockSpec((per_step, lags, width), lambda s: (s, 0, 0))],
-        out_specs=pl.BlockSpec((2, 2 * per_step, channels, lags), lambda s: (0, s, 0, 0)),
-        compiler_params=pltpu.CompilerParams(vmem_limit_bytes=24 * 2**20),
-        name="finish",
-    )(sums)
     return out.reshape(1, channels, channels, lags)
 
 
@@ -341,9 +337,11 @@
     whitened = whiten(spectra)
     length_bins = spectra.shape[3]
     reach = pair_blocks.shape[0] * wins // 2
-    table = jnp.asarray(make_table(length_bins))
+    chunks = 8 if wins <= 2 * CORES else 4
+    table = make_table(length_bins).reshape(NLAG, 2, chunks, -1).transpose(0, 2, 1, 3)
+    table = jnp.asarray(table.reshape(NLAG, 2 * length_bins))
     scaling = 1.0 / math.sqrt(spectra.shape[1] * wins * length_bins)
-    return finish(spread(pair_blocks, arrange(whitened), table, reach, chans, wins), scaling)
+    return spread(pair_blocks, arrange(whitened), table, scaling, reach, chans, wins, chunks)
 
 
 def solution(mesh):

time: 77.3 us -> 70.2 us (0.908)
  Pallas kernels: 71.5 us -> 61.8 us
  local copies, waits for them, and re-layouts: 2.97 us -> 5.49 us
    pallas_call x1, Pallas kernels: 66.2 us -> 60.8 us  [spread(): pl.pallas_call(functools.partial(spread_kernel, reach, chans, wins, chunk...]
    pallas_call x1 -> x0, Pallas kernels: 4.19 us -> none  [finish(): pl.pallas_call(functools.partial(finish_kernel, scaling), out_shape=jax.S...]
    unnamed x6 -> x5, local copies, waits for them, and re-layouts: 2.97 us -> 5.49 us
where the time goes in v2:
time: 70.2 us; the launch traced here: 70 us
  Pallas kernels  61.8 us (88%)
  local copies, waits for them, and re-layouts  5.49 us (8%)
  other arithmetic  1.52 us (2%)
  matrix products  1.09 us (2%)
    pallas_call x1, Pallas kernels, spread(): pl.pallas_call(functools.partial(spread_kernel, reach, chans, wins, chunk...  60.8 us
    unnamed x5, local copies, waits for them, and re-layouts  5.49 us

profile of v2, /device:TPU:0, one launch (start us, length us, event | category | flops | bytes accessed | tf_op | source)
XLA Modules:
  0.0 70.0 jit_solution(9691352103017808191)
XLA Ops:
  0.0 0.0 copy-start.1
  0.0 0.2 convert_reduce_fusion
  0.2 1.1 %fusion.5 = f32[1,2,64,1024]{3,2,1,0:T(8,128)S(1)} fusion(bf16[2,2,64,1024]{3,2,1,0:T(8,128)(2,1)} %param.3), kind=kLoop, calls=%fused_computation.11 | loop fusion | flops 655360 | bytes 1048576 | tf_op jit(solution)/shard_map/add | solution.py:35
  1.3 1.1 %fusion.4 = f32[128,1024]{1,0:T(8,128)S(1)} fusion(f32[128,1024]{1,0:T(8,128)S(1)} %bitcast.8, f32[1024]{0:T(1024)S(1)} %convert_reduce_fusion), kind=kOutput, calls=%fused_computation.6 | convolution fusion | flops 1614020608 | bytes 1052672 | tf_op jit(solution)/shard_map/dot_general | solution.py:39
  2.4 0.0 copy-done.1
  2.5 0.1 fusion.6
  2.6 0.1 pad_maximum_fusion
  2.7 1.1 %arrange.1.p_ref = bf16[32,64,128]{2,1,0:T(8,128)(2,1)S(1)} custom-call(bf16[4,64,1024]{2,1,0:T(8,128)(2,1)S(1)} %bitcast.5), custom_call_target="tpu_custom_call" | custom-call | tf_op jit(solution)/shard_map/arrange/pallas_call | solution.py:76
  3.7 0.0 copy-start
  3.7 0.8 %copy-done = bf16[32,64,128]{2,1,0:T(8,128)(2,1)} copy-done((bf16[32,64,128]{2,1,0:T(8,128)(2,1)}, bf16[32,64,128]{2,1,0:T(8,128)(2,1)S(1)}, u32[]{:S(2)}) %copy-start) | copy-done | bytes 524312
  4.5 60.8 %spread.1 = f32[2,32,64,256]{3,2,1,0:T(8,128)} custom-call(s32[1,2]{1,0:T(1,128)} %pair_ref.1, bf16[32,64,128]{2,1,0:T(8,128)(2,1)} %copy-done, bf16[256,2048]{1,0:T(8,128)(2,1)} %constant.8.clone.t_ref), custom_call_target="tpu_custom_call" | custom-call | tf_op jit(solution)/shard_map/spread/pallas_call | solution.py:320
  65.3 4.7 %copy.5 = f32[1,64,64,256]{3,2,1,0:T(8,128)} copy(f32[1,64,64,256]{3,2,1,0:T(8,128)} %bitcast.6) | data formatting | bytes 8388608
Async XLA Ops:
  0.0 2.4 %copy-start.1 = (bf16[2,2,64,1024]{3,2,1,0:T(8,128)(2,1)S(1)}, bf16[2,2,64,1024]{3,2,1,0:T(8,128)(2,1)}, u32[]{:S(2)}) copy-start(bf16[2,2,64,1024]{3,2,1,0:T(8,128)(2,1)} %param.3) | copy-start | bytes 1572868
  3.7 0.8 %copy-start = (bf16[32,64,128]{2,1,0:T(8,128)(2,1)}, bf16[32,64,128]{2,1,0:T(8,128)(2,1)S(1)}, u32[]{:S(2)}) copy-start(bf16[32,64,128]{2,1,0:T(8,128)(2,1)S(1)} %arrange.1.p_ref) | copy-start | bytes 1572868

commit v3 on v2

--- a/solution.py
+++ b/solution.py
@@ -135,7 +135,7 @@
     lax.fori_loop(0, groups, group_step, 0, unroll=2)
 
 
-def lag_chunk(ch, chunks, scaling, t_ref, cross, sums, send):
+def lag_chunk(ch, chunks, t_ref, cross, sums, send):
     count, quarters, channels, width = sums.shape
     size = 2 * cross.shape[2]
 
@@ -147,7 +147,7 @@
         if ch:
             total = total + sums[p].reshape(quarters * channels, width)
         if ch == chunks - 1:
-            total = (total * scaling).T
+            total = total.T
         sums[p] = total.reshape(quarters, channels, width)
         if ch == chunks - 1:
             for n in range(quarters):
@@ -157,7 +157,7 @@
     lax.fori_loop(0, count, pair_step, 0, unroll=2)
 
 
-def spread_kernel(reach, chans, wins, chunks, scaling, pair_ref, p_ref, t_ref, o_ref, cross, sums,
+def spread_kernel(reach, chans, wins, chunks, pair_ref, p_ref, t_ref, o_ref, cross, sums,
                   out_sem, own_sem, s1, r1, s2, r2, s3, r3, *bufs):
     chan = lax.axis_index("chan")
     win = lax.axis_index("win")
@@ -277,19 +277,22 @@
             for step in range(rows):
                 from_beside(o + own, step, ch).wait_recv()
         cross_chunk(pick, bufs[ch], cross)
-        lag_chunk(ch, chunks, scaling, t_ref, cross, sums, send)
-
-    begin(0)
-    begin(1)
-    for ch in range(chunks + 2):
+        lag_chunk(ch, chunks, t_ref, cross, sums, send)
+
+    ahead = 3
+    for ch in range(ahead):
+        begin(ch)
+    for ch in range(chunks + ahead):
         if ch < chunks:
             second(ch)
-        if ch + 2 < chunks:
-            begin(ch + 2)
-        if 0 <= ch - 1 < chunks:
-            third(ch - 1)
-        if ch - 2 >= 0:
-            compute(ch - 2)
+        if ch + ahead < chunks:
+            begin(ch + ahead)
+        if ch == chunks + 1:
+            compute(ch - ahead)
+        if 0 <= ch - 2 < chunks:
+            third(ch - 2)
+        if ch >= ahead and ch != chunks + 1:
+            compute(ch - ahead)
     for ch in range(chunks):
         for o in offsets:
             for step in range(rows):
@@ -318,7 +321,7 @@
     buf = pltpu.VMEM((slots, wins, size, channels, lanes), piece.dtype)
     vmem = pl.BlockSpec(memory_space=pltpu.VMEM)
     out = pl.pallas_call(
-        functools.partial(spread_kernel, reach, chans, wins, chunks, scaling),
+        functools.partial(spread_kernel, reach, chans, wins, chunks),
         out_shape=jax.ShapeDtypeStruct((2, half, channels, lags), jnp.float32),
         in_specs=[pl.BlockSpec(memory_space=pltpu.SMEM), vmem, vmem],
         out_specs=pl.BlockSpec(memory_space=pl.ANY),
@@ -330,7 +333,7 @@
             collective_id=0, has_side_effects=True, vmem_limit_bytes=56 * 2**20),
         name="spread",
     )(pairs, piece, table)
-    return out.reshape(1, channels, channels, lags)
+    return out.reshape(1, channels, channels, lags) * scaling
 
 
 def per_device(chans, wins, spectra, pair_blocks):

time: 70.2 us -> 71.2 us (1.014); the launches traced: 70 us -> 70.1 us
  other arithmetic: 1.52 us -> 6.48 us
  local copies, waits for them, and re-layouts: 5.49 us -> 0.79 us
    mul x0 -> x1, other arithmetic: none -> 4.95 us  [spread(): return out.reshape(1, channels, channels, lags) * scaling]
    unnamed x5 -> x4, local copies, waits for them, and re-layouts: 5.49 us -> 0.79 us
where the time goes in v3:
time: 71.2 us; the launch traced here: 70.1 us
  Pallas kernels  61.7 us (87%)
  other arithmetic  6.48 us (9%)
  matrix products  1.09 us (2%)
  local copies, waits for them, and re-layouts  0.79 us (1%)
    pallas_call x1, Pallas kernels, spread(): pl.pallas_call(functools.partial(spread_kernel, reach, chans, wins, chunk...  60.6 us
    mul x1, other arithmetic, spread(): return out.reshape(1, channels, channels, lags) * scaling  4.95 us

profile of v3, /device:TPU:0, one launch (start us, length us, event | category | flops | bytes accessed | tf_op | source)
XLA Modules:
  0.0 70.1 jit_solution(16182118653009127510)
XLA Ops:
  0.0 0.0 copy-start.1
  0.0 0.2 convert_reduce_fusion
  0.2 1.1 %fusion.5 = f32[1,2,64,1024]{3,2,1,0:T(8,128)S(1)} fusion(bf16[2,2,64,1024]{3,2,1,0:T(8,128)(2,1)} %param.3), kind=kLoop, calls=%fused_computation.12 | loop fusion | flops 655360 | bytes 1048576 | tf_op jit(solution)/shard_map/add | solution.py:35
  1.3 1.1 %fusion.4 = f32[128,1024]{1,0:T(8,128)S(1)} fusion(f32[128,1024]{1,0:T(8,128)S(1)} %bitcast.7, f32[1024]{0:T(1024)S(1)} %convert_reduce_fusion), kind=kOutput, calls=%fused_computation.7 | convolution fusion | flops 1614020608 | bytes 1052672 | tf_op jit(solution)/shard_map/dot_general | solution.py:39
  2.4 0.0 copy-done.1
  2.5 0.1 fusion.6
  2.6 0.1 pad_maximum_fusion
  2.7 1.1 %arrange.1.p_ref = bf16[32,64,128]{2,1,0:T(8,128)(2,1)S(1)} custom-call(bf16[4,64,1024]{2,1,0:T(8,128)(2,1)S(1)} %bitcast.5), custom_call_target="tpu_custom_call" | custom-call | tf_op jit(solution)/shard_map/arrange/pallas_call | solution.py:76
  3.7 0.0 copy-start
  3.7 0.8 %copy-done = bf16[32,64,128]{2,1,0:T(8,128)(2,1)} copy-done((bf16[32,64,128]{2,1,0:T(8,128)(2,1)}, bf16[32,64,128]{2,1,0:T(8,128)(2,1)S(1)}, u32[]{:S(2)}) %copy-start) | copy-done | bytes 524312
  4.5 60.6 %spread.1 = f32[2,32,64,256]{3,2,1,0:T(8,128)} custom-call(s32[1,2]{1,0:T(1,128)} %pair_ref.1, bf16[32,64,128]{2,1,0:T(8,128)(2,1)} %copy-done, bf16[256,2048]{1,0:T(8,128)(2,1)} %constant.10.clone.t_ref), custom_call_target="tpu_custom_call" | custom-call | tf_op jit(solution)/shard_map/spread/pallas_call | solution.py:323
  65.1 5.0 %broadcast_multiply_fusion = f32[2,32,64,256]{3,2,1,0:T(8,128)} fusion(f32[2,32,64,256]{3,2,1,0:T(8,128)} %spread.1), kind=kLoop, calls=%fused_computation.3 | loop fusion | flops 1048576 | bytes 8388608 | tf_op jit(solution)/shard_map/mul | solution.py:336
Async XLA Ops:
  0.0 2.4 %copy-start.1 = (bf16[2,2,64,1024]{3,2,1,0:T(8,128)(2,1)S(1)}, bf16[2,2,64,1024]{3,2,1,0:T(8,128)(2,1)}, u32[]{:S(2)}) copy-start(bf16[2,2,64,1024]{3,2,1,0:T(8,128)(2,1)} %param.3) | copy-start | bytes 1572868
  3.7 0.8 %copy-start = (bf16[32,64,128]{2,1,0:T(8,128)(2,1)}, bf16[32,64,128]{2,1,0:T(8,128)(2,1)S(1)}, u32[]{:S(2)}) copy-start(bf16[32,64,128]{2,1,0:T(8,128)(2,1)S(1)} %arrange.1.p_ref) | copy-start | bytes 1572868

commit v4 on v2

--- a/solution.py
+++ b/solution.py
@@ -88,7 +88,7 @@
     _, wins, groups, channels, lanes = buf.shape
     half = channels // 2
     lane = lax.broadcasted_iota(jnp.int32, (1, lanes), 1)
-    place = (lane // TILE) % QUADS
+    place = (lax.broadcasted_iota(jnp.int32, (channels, lanes), 1) // TILE) % QUADS
     keep = lax.broadcasted_iota(jnp.int32, (2 * TILE, lanes), 0) % TILE == lax.broadcasted_iota(
         jnp.int32, (2 * TILE, lanes), 1) % TILE
     keep = keep.astype(jnp.float32).astype(jnp.bfloat16)[None]
@@ -101,23 +101,23 @@
             out = jnp.where(place == (m + quad) % QUADS, pieces[m], out)
         return out
 
+
     def spread_rows(x):
         wide = jnp.broadcast_to(x[:, None, :], (half, TILE, lanes))
         wide = wide.reshape(half * TILE // (2 * TILE), 2 * TILE, lanes).astype(jnp.bfloat16) * keep
         return wide.reshape(half * TILE, lanes)
 
     def group_step(group, carry):
-        a_pieces = [buf[pick[0], m, group].astype(jnp.float32) for m in range(wins)]
-        b_pieces = [buf[pick[1], m, group].astype(jnp.float32) for m in range(wins)]
+        a_pieces = [buf[pick[0], m, group] for m in range(wins)]
+        b_pieces = [buf[pick[1], m, group] for m in range(wins)]
         for pair in range(QUADS // 2):
             both = []
             for quad in (2 * pair, 2 * pair + 1):
                 total = None
                 for bundle in range(0, wins, QUADS):
-                    a = merged(a_pieces[bundle:bundle + QUADS], quad)
+                    a = merged(a_pieces[bundle:bundle + QUADS], quad).astype(jnp.float32)
                     b = merged(b_pieces[bundle:bundle + QUADS], quad)
-                    bx = (pltpu.roll(b, lanes // 2, 1) * sign).astype(jnp.bfloat16)
-                    b = b.astype(jnp.bfloat16)
+                    bx = (pltpu.roll(b.astype(jnp.float32), lanes // 2, 1) * sign).astype(jnp.bfloat16)
                     left = jnp.concatenate([spread_rows(a[:half]), spread_rows(a[half:])], axis=1)
                     right = jnp.concatenate(
                         [jnp.concatenate([b, zero, bx, zero], axis=0),
@@ -135,7 +135,7 @@
     lax.fori_loop(0, groups, group_step, 0, unroll=2)
 
 
-def lag_chunk(ch, chunks, scaling, t_ref, cross, sums, send):
+def lag_chunk(ch, chunks, t_ref, cross, sums, send):
     count, quarters, channels, width = sums.shape
     size = 2 * cross.shape[2]
 
@@ -147,7 +147,7 @@
         if ch:
             total = total + sums[p].reshape(quarters * channels, width)
         if ch == chunks - 1:
-            total = (total * scaling).T
+            total = total.T
         sums[p] = total.reshape(quarters, channels, width)
         if ch == chunks - 1:
             for n in range(quarters):
@@ -157,7 +157,7 @@
     lax.fori_loop(0, count, pair_step, 0, unroll=2)
 
 
-def spread_kernel(reach, chans, wins, chunks, scaling, pair_ref, p_ref, t_ref, o_ref, cross, sums,
+def spread_kernel(reach, chans, wins, chunks, pair_ref, p_ref, t_ref, o_ref, cross, sums,
                   out_sem, own_sem, s1, r1, s2, r2, s3, r3, *bufs):
     chan = lax.axis_index("chan")
     win = lax.axis_index("win")
@@ -277,7 +277,7 @@
             for step in range(rows):
                 from_beside(o + own, step, ch).wait_recv()
         cross_chunk(pick, bufs[ch], cross)
-        lag_chunk(ch, chunks, scaling, t_ref, cross, sums, send)
+        lag_chunk(ch, chunks, t_ref, cross, sums, send)
 
     begin(0)
     begin(1)
@@ -318,7 +318,7 @@
     buf = pltpu.VMEM((slots, wins, size, channels, lanes), piece.dtype)
     vmem = pl.BlockSpec(memory_space=pltpu.VMEM)
     out = pl.pallas_call(
-        functools.partial(spread_kernel, reach, chans, wins, chunks, scaling),
+        functools.partial(spread_kernel, reach, chans, wins, chunks),
         out_shape=jax.ShapeDtypeStruct((2, half, channels, lags), jnp.float32),
         in_specs=[pl.BlockSpec(memory_space=pltpu.SMEM), vmem, vmem],
         out_specs=pl.BlockSpec(memory_space=pl.ANY),
@@ -330,7 +330,24 @@
             collective_id=0, has_side_effects=True, vmem_limit_bytes=56 * 2**20),
         name="spread",
     )(pairs, piece, table)
-    return out.reshape(1, channels, channels, lags)
+    return scale(out, scaling).reshape(1, channels, channels, lags)
+
+
+def scale_kernel(scaling, x_ref, o_ref):
+    o_ref[...] = x_ref[...] * scaling
+
+
+def scale(x, scaling):
+    block = pl.BlockSpec((1, x.shape[1] // 4) + x.shape[2:], lambda h, s: (h, s, 0, 0))
+    return pl.pallas_call(
+        functools.partial(scale_kernel, scaling),
+        out_shape=jax.ShapeDtypeStruct(x.shape, x.dtype),
+        grid=(x.shape[0], 4),
+        in_specs=[block],
+        out_specs=block,
+        compiler_params=pltpu.CompilerParams(vmem_limit_bytes=60 * 2**20),
+        name="scale",
+    )(x)
 
 
 def per_device(chans, wins, spectra, pair_blocks):

time: 70.2 us -> 72.3 us (1.030)
  Pallas kernels: 61.8 us -> 68.6 us
  local copies, waits for them, and re-layouts: 5.49 us -> 0.79 us
    pallas_call x0 -> x1, Pallas kernels: none -> 6.64 us  [scale(): pl.pallas_call(functools.partial(scale_kernel, scaling), out_shape=jax.Sh...]
    unnamed x5 -> x4, local copies, waits for them, and re-layouts: 5.49 us -> 0.79 us
where the time goes in v4:
time: 72.3 us; the launch traced here: 72 us
  Pallas kernels  68.6 us (95%)
  other arithmetic  1.52 us (2%)
  matrix products  1.09 us (2%)
  local copies, waits for them, and re-layouts  0.79 us (1%)
    pallas_call x1, Pallas kernels, spread(): pl.pallas_call(functools.partial(spread_kernel, reach, chans, wins, chunk...  60.9 us
    pallas_call x1, Pallas kernels, scale(): pl.pallas_call(functools.partial(scale_kernel, scaling), out_shape=jax.Sh...  6.64 us

profile of v4, /device:TPU:0, one launch (start us, length us, event | category | flops | bytes accessed | tf_op | source)
XLA Modules:
  0.0 72.0 jit_solution(16833512194620019543)
XLA Ops:
  0.0 0.0 copy-start.1
  0.0 0.2 convert_reduce_fusion
  0.2 1.1 %fusion.5 = f32[1,2,64,1024]{3,2,1,0:T(8,128)S(1)} fusion(bf16[2,2,64,1024]{3,2,1,0:T(8,128)(2,1)} %param.3), kind=kLoop, calls=%fused_computation.11 | loop fusion | flops 655360 | bytes 1048576 | tf_op jit(solution)/shard_map/add | solution.py:35
  1.3 1.1 %fusion.4 = f32[128,1024]{1,0:T(8,128)S(1)} fusion(f32[128,1024]{1,0:T(8,128)S(1)} %bitcast.7, f32[1024]{0:T(1024)S(1)} %convert_reduce_fusion), kind=kOutput, calls=%fused_computation.6 | convolution fusion | flops 1614020608 | bytes 1052672 | tf_op jit(solution)/shard_map/dot_general | solution.py:39
  2.4 0.0 copy-done.1
  2.5 0.1 fusion.6
  2.6 0.1 pad_maximum_fusion
  2.7 1.1 %arrange.1.p_ref = bf16[32,64,128]{2,1,0:T(8,128)(2,1)S(1)} custom-call(bf16[4,64,1024]{2,1,0:T(8,128)(2,1)S(1)} %bitcast.5), custom_call_target="tpu_custom_call" | custom-call | tf_op jit(solution)/shard_map/arrange/pallas_call | solution.py:76
  3.7 0.0 copy-start
  3.7 0.8 %copy-done = bf16[32,64,128]{2,1,0:T(8,128)(2,1)} copy-done((bf16[32,64,128]{2,1,0:T(8,128)(2,1)}, bf16[32,64,128]{2,1,0:T(8,128)(2,1)S(1)}, u32[]{:S(2)}) %copy-start) | copy-done | bytes 524312
  4.5 60.9 %spread.1.x_ref = f32[2,32,64,256]{3,2,1,0:T(8,128)} custom-call(s32[1,2]{1,0:T(1,128)} %pair_ref.1, bf16[32,64,128]{2,1,0:T(8,128)(2,1)} %copy-done, bf16[256,2048]{1,0:T(8,128)(2,1)} %constant.8.clone.t_ref), custom_call_target="tpu_custom_call" | custom-call | tf_op jit(solution)/shard_map/spread/pallas_call | solution.py:320
  65.4 6.6 %scale.1 = f32[2,32,64,256]{3,2,1,0:T(8,128)} custom-call(f32[2,32,64,256]{3,2,1,0:T(8,128)} %spread.1.x_ref), custom_call_target="tpu_custom_call" | custom-call | tf_op jit(solution)/shard_map/scale/pallas_call | solution.py:342
Async XLA Ops:
  0.0 2.4 %copy-start.1 = (bf16[2,2,64,1024]{3,2,1,0:T(8,128)(2,1)S(1)}, bf16[2,2,64,1024]{3,2,1,0:T(8,128)(2,1)}, u32[]{:S(2)}) copy-start(bf16[2,2,64,1024]{3,2,1,0:T(8,128)(2,1)} %param.3) | copy-start | bytes 1572868
  3.7 0.8 %copy-start = (bf16[32,64,128]{2,1,0:T(8,128)(2,1)}, bf16[32,64,128]{2,1,0:T(8,128)(2,1)S(1)}, u32[]{:S(2)}) copy-start(bf16[32,64,128]{2,1,0:T(8,128)(2,1)S(1)} %arrange.1.p_ref) | copy-start | bytes 1572868

commit v5 on v2

--- a/solution.py
+++ b/solution.py
@@ -157,8 +157,8 @@
     lax.fori_loop(0, count, pair_step, 0, unroll=2)
 
 
-def spread_kernel(reach, chans, wins, chunks, scaling, pair_ref, p_ref, t_ref, o_ref, cross, sums,
-                  out_sem, own_sem, s1, r1, s2, r2, s3, r3, *bufs):
+def spread_kernel(reach, chans, wins, chunks, scaling, pair_ref, p_ref, table_ref, o_ref, cross, sums,
+                  t_ref, t_sem, out_sem, own_sem, s1, r1, s2, r2, s3, r3, *bufs):
     chan = lax.axis_index("chan")
     win = lax.axis_index("win")
     row = win // CORES
@@ -188,6 +188,9 @@
     def mine(ch):
         return pltpu.make_async_copy(origin(own, 0, ch), place(own, win, ch), own_sem.at[ch])
 
+    table = pltpu.make_async_copy(table_ref, t_ref, t_sem)
+    table.start()
+
     def place(slot, piece, ch):
         return bufs[ch].at[slot, piece]
 
@@ -197,7 +200,7 @@
         return place(slot, peer(-step), ch)
 
     def whole_way(o, ch):
-        return abs(o) == 1 and ch % 2 == 0
+        return ch % 3 == min(abs(o), 2) or ch == chunks - 1
 
     def along(o, step, ch):
         slot = o + own
@@ -272,6 +275,8 @@
             for n in range(2)]
 
     def compute(ch):
+        if ch == 0:
+            table.wait()
         mine(ch).wait()
         for o in offsets:
             for step in range(rows):
@@ -320,10 +325,13 @@
     out = pl.pallas_call(
         functools.partial(spread_kernel, reach, chans, wins, chunks, scaling),
         out_shape=jax.ShapeDtypeStruct((2, half, channels, lags), jnp.float32),
-        in_specs=[pl.BlockSpec(memory_space=pltpu.SMEM), vmem, vmem],
+        in_specs=[pl.BlockSpec(memory_space=pltpu.SMEM), vmem,
+                  pl.BlockSpec(memory_space=pl.ANY)],
         out_specs=pl.BlockSpec(memory_space=pl.ANY),
         scratch_shapes=[pltpu.VMEM((half, 2, bins // chunks, 2 * channels), jnp.bfloat16),
                         pltpu.VMEM((half // 2, 4, channels, lags), jnp.float32),
+                        pltpu.VMEM(table.shape, table.dtype),
+                        pltpu.SemaphoreType.DMA,
                         pltpu.SemaphoreType.DMA((half // 2, 4)),
                         pltpu.SemaphoreType.DMA((chunks,))] + [sems] * 6 + [buf] * chunks,
         compiler_params=pltpu.CompilerParams(

time: 70.2 us -> 68.1 us (0.970)
  Pallas kernels: 61.8 us -> 59.8 us
    pallas_call x1, Pallas kernels: 60.8 us -> 58.7 us  [spread(): pl.pallas_call(functools.partial(spread_kernel, reach, chans, wins, chunk...]
where the time goes in v5:
time: 68.1 us; the launch traced here: 67.9 us
  Pallas kernels  59.8 us (88%)
  local copies, waits for them, and re-layouts  5.49 us (8%)
  other arithmetic  1.52 us (2%)
  matrix products  1.09 us (2%)
    pallas_call x1, Pallas kernels, spread(): pl.pallas_call(functools.partial(spread_kernel, reach, chans, wins, chunk...  58.7 us
    unnamed x5, local copies, waits for them, and re-layouts  5.49 us

profile of v5, /device:TPU:0, one launch (start us, length us, event | category | flops | bytes accessed | tf_op | source)
XLA Modules:
  0.0 67.9 jit_solution(9877237270274848666)
XLA Ops:
  0.0 0.0 copy-start.1
  0.0 0.2 convert_reduce_fusion
  0.2 1.1 %fusion.5 = f32[1,2,64,1024]{3,2,1,0:T(8,128)S(1)} fusion(bf16[2,2,64,1024]{3,2,1,0:T(8,128)(2,1)} %param.3), kind=kLoop, calls=%fused_computation.11 | loop fusion | flops 655360 | bytes 1048576 | tf_op jit(solution)/shard_map/add | solution.py:35
  1.3 1.1 %fusion.4 = f32[128,1024]{1,0:T(8,128)S(1)} fusion(f32[128,1024]{1,0:T(8,128)S(1)} %bitcast.8, f32[1024]{0:T(1024)S(1)} %convert_reduce_fusion), kind=kOutput, calls=%fused_computation.6 | convolution fusion | flops 1614020608 | bytes 1052672 | tf_op jit(solution)/shard_map/dot_general | solution.py:39
  2.4 0.0 copy-done.1
  2.5 0.1 fusion.6
  2.6 0.1 pad_maximum_fusion
  2.7 1.1 %arrange.1.p_ref = bf16[32,64,128]{2,1,0:T(8,128)(2,1)S(1)} custom-call(bf16[4,64,1024]{2,1,0:T(8,128)(2,1)S(1)} %bitcast.5), custom_call_target="tpu_custom_call" | custom-call | tf_op jit(solution)/shard_map/arrange/pallas_call | solution.py:76
  3.7 0.0 copy-start
  3.7 0.8 %copy-done = bf16[32,64,128]{2,1,0:T(8,128)(2,1)} copy-done((bf16[32,64,128]{2,1,0:T(8,128)(2,1)}, bf16[32,64,128]{2,1,0:T(8,128)(2,1)S(1)}, u32[]{:S(2)}) %copy-start) | copy-done | bytes 524312
  4.5 58.7 %spread.1 = f32[2,32,64,256]{3,2,1,0:T(8,128)} custom-call(s32[1,2]{1,0:T(1,128)} %pair_ref.1, bf16[32,64,128]{2,1,0:T(8,128)(2,1)} %copy-done, bf16[256,2048]{1,0:T(8,128)(2,1)} %constant.8.clone.table_ref), custom_call_target="tpu_custom_call" | custom-call | tf_op jit(solution)/shard_map/spread/pallas_call | solution.py:325
  63.2 4.7 %copy.5 = f32[1,64,64,256]{3,2,1,0:T(8,128)} copy(f32[1,64,64,256]{3,2,1,0:T(8,128)} %bitcast.6) | data formatting | bytes 8388608
Async XLA Ops:
  0.0 2.4 %copy-start.1 = (bf16[2,2,64,1024]{3,2,1,0:T(8,128)(2,1)S(1)}, bf16[2,2,64,1024]{3,2,1,0:T(8,128)(2,1)}, u32[]{:S(2)}) copy-start(bf16[2,2,64,1024]{3,2,1,0:T(8,128)(2,1)} %param.3) | copy-start | bytes 1572868
  3.7 0.8 %copy-start = (bf16[32,64,128]{2,1,0:T(8,128)(2,1)}, bf16[32,64,128]{2,1,0:T(8,128)(2,1)S(1)}, u32[]{:S(2)}) copy-start(bf16[32,64,128]{2,1,0:T(8,128)(2,1)S(1)} %arrange.1.p_ref) | copy-start | bytes 1572868
